TPU v7x, 32 devices: a whole 2x2x4 slice. The times are simulated.
32 devices in a mesh: section: 4 (over y, core), seq: 8 (over z, x).
Axes of the slice: x: 2, y: 2, z: 4, core: 2. Of those that a mesh axis runs over, the one named last changes fastest.
Arguments:
- queries: bfloat16 [4, 1024, 1024], P('section', 'seq'), may hold values from -15 to 15, as said below
- keys: bfloat16 [4, 1024, 128], P('section', 'seq'), may hold values from -6 to 6, as said below
- values: bfloat16 [4, 1024, 128], P('section', 'seq'), may hold values from -6 to 6
- cache_keys: bfloat16 [4, 8, 512, 128], P('section', 'seq'), may hold values from -6 to 6
- cache_values: bfloat16 [4, 8, 512, 128], P('section', 'seq'), may hold values from -6 to 6
- vertical: int32 [4, 8, 32], P('section', 'seq'), may hold values from 0 to 63, as said below
- vertical_count: int32 [4, 8], P('section', 'seq'), may hold values from 1 to 32, as said below
- slash: int32 [4, 8, 11], P('section', 'seq'), may hold values from 1 to 79, as said below
Outputs:
- attended: bfloat16 [4, 1024, 1024], P('section', 'seq')
Inputs may be any that keep to these rules, and one draw needn't show every extreme that they name: queries within the range in both draws. keys within the range in both draws. `vertical`: for each layer and head, the 32 entries are distinct cached block indices. `vertical_count`: in every layer some head uses all 32 slots. `slash`: for each layer and head, the 11 offsets are distinct.
All inputs are finite; a program needn't handle non-finite values.
Results may differ from a plain program's by a relative error of at most 0.011.
Values may be sent and summed in bfloat16 or wider, within the bound.
A program may use at most 64 MiB of HBM per device.

v0:
```python
import math

import jax
import jax.numpy as jnp
from jax import lax
from jax.sharding import PartitionSpec as P

HEAD_SIZE = 128
GROUP = 8
BLK = 64
TILE = 4
NVMAX = 32
NS = 11
CACHE = 4096


big_negative = -1e30


def from_partner(value, axis, distance):
    mask = 2**distance
    pairs = [(source, source ^ mask) for source in range(lax.axis_size(axis))]
    return lax.ppermute(value, axis, pairs)


def from_behind(x, axis, by):
    peers = lax.axis_size(axis)
    return lax.ppermute(x, axis, [(i, (i + by) % peers) for i in range(peers)])


def online_update(carry, scores, allowed, contract):
    top, total, accum = carry
    masked = jnp.where(allowed, scores, big_negative)
    new_top = jnp.maximum(top, jnp.max(masked, axis=-1))
    factor = jnp.exp(top - new_top)
    attention_weight = jnp.where(allowed, jnp.exp(scores - new_top[..., None]), 0.0)
    total = total * factor + jnp.sum(attention_weight, axis=-1)
    accum = accum * factor[..., None] + contract(attention_weight.astype(jnp.bfloat16))
    return (new_top, total, accum)


def vertical_run(query_matrix, verts, count, first_tile, last_tile, all_kv, carry):
    softmax_scale = 1.0 / math.sqrt(HEAD_SIZE)
    span = TILE * BLK
    slot_ids = jnp.arange(TILE, dtype=jnp.int32)
    block_view = all_kv.reshape(all_kv.shape[0] // BLK, BLK, 2 * HEAD_SIZE)

    def step(tile, state):
        picked = lax.dynamic_slice_in_dim(verts, tile * TILE, TILE)
        kv_tile = jnp.take(block_view, picked, axis=0).reshape(span, 2 * HEAD_SIZE)
        key_tile = kv_tile[:, :HEAD_SIZE]
        value_tile = kv_tile[:, HEAD_SIZE:]
        live = jnp.repeat(tile * TILE + slot_ids < count, BLK)
        scores = (
            lax.dot_general(
                query_matrix, key_tile, (((1,), (1,)), ((), ())), preferred_element_type=jnp.float32
            )
            * softmax_scale
        )

        def contract(attention_weight):
            return jnp.dot(attention_weight, value_tile, preferred_element_type=jnp.float32)

        return online_update(state, scores, live[None, :], contract)

    return lax.fori_loop(first_tile, last_tile, step, carry)


def slash_run(query_matrix, verts, count, slashes, all_kv, carry):
    softmax_scale = 1.0 / math.sqrt(HEAD_SIZE)
    prefill_stretch = query_matrix.shape[0]
    ncb = CACHE // BLK
    nqb = prefill_stretch // BLK
    per = math.gcd(nqb, max(1, 512 // BLK))
    rounds = nqb // per
    width = (NS + 1) * BLK
    inner = jnp.arange(BLK, dtype=jnp.int32)
    offsets = jnp.concatenate([jnp.zeros((1,), jnp.int32), slashes])
    blocks = ncb + jnp.arange(nqb, dtype=jnp.int32)[:, None] - offsets[None, :]
    used = jnp.arange(NVMAX, dtype=jnp.int32)[None, None, :] < count
    listed = jnp.any((blocks[:, :, None] == verts[None, None, :]) & used, axis=2)
    valid = (blocks >= 0) & jnp.logical_not(listed)
    column = jnp.arange(width, dtype=jnp.int32)
    causal = (column[None, :] >= BLK) | ((column % BLK)[None, :] <= inner[:, None])
    padded = jnp.concatenate(
        [jnp.zeros((prefill_stretch, 2 * HEAD_SIZE), all_kv.dtype), all_kv], axis=0
    )
    starts = (nqb + ncb - offsets) * BLK
    top, total, accum = carry

    def one_round(items):
        round_id, local_query_share, valid_part, top_part, total_part, accum_part = items
        base = round_id * (per * BLK)

        def cut(start_row):
            return lax.dynamic_slice_in_dim(padded, start_row + base, per * BLK, 0)

        slabs = jax.vmap(cut)(starts)
        shares = (
            slabs.reshape(NS + 1, per, BLK, 2 * HEAD_SIZE)
            .transpose(1, 0, 2, 3)
            .reshape(per, width, 2 * HEAD_SIZE)
        )
        local_key_share = shares[:, :, :HEAD_SIZE]
        local_value_share = shares[:, :, HEAD_SIZE:]
        scores = (
            jnp.einsum(
                "cra,cma->crm",
                local_query_share,
                local_key_share,
                preferred_element_type=jnp.float32,
            )
            * softmax_scale
        )
        allowed = jnp.repeat(valid_part, BLK, axis=1)[:, None, :] & causal[None, :, :]

        def contract(attention_weight):
            return jnp.einsum(
                "owu,out->owt",
                attention_weight,
                local_value_share,
                preferred_element_type=jnp.float32,
            )

        return online_update((top_part, total_part, accum_part), scores, allowed, contract)

    items = (
        jnp.arange(rounds, dtype=jnp.int32),
        query_matrix.reshape(rounds, per, BLK, HEAD_SIZE),
        valid.reshape(rounds, per, NS + 1),
        top.reshape(rounds, per, BLK),
        total.reshape(rounds, per, BLK),
        accum.reshape(rounds, per, BLK, HEAD_SIZE),
    )
    new_top, new_total, new_accum = lax.map(one_round, items)
    return (
        new_top.reshape(prefill_stretch),
        new_total.reshape(prefill_stretch),
        new_accum.reshape(prefill_stretch, HEAD_SIZE),
    )


def assemble(piece, bits, rank):
    for bit in range(bits):
        other = from_partner(piece, "seq", bit)
        upper = rank // 2**bit % 2 == 1
        lower_half = jnp.where(upper, other, piece)
        upper_half = jnp.where(upper, piece, other)
        piece = jnp.concatenate([lower_half, upper_half], axis=0)
    return piece


def per_device(queries, keys, values, cache_keys, cache_values, vertical, vertical_count, slash):
    query_rows, key_rows, value_rows = from_behind((queries, keys, values), "section", 1)
    tok = query_rows.shape[1]
    heads = lax.axis_size("seq")
    kv_heads = key_rows.shape[2] // HEAD_SIZE
    prefill_stretch = tok * heads
    bits = GROUP.bit_length() - 1
    rank = lax.axis_index("seq")
    q_rows = query_rows[0].reshape(tok, heads, HEAD_SIZE)
    kv_rows = jnp.concatenate(
        [
            key_rows[0].reshape(tok, kv_heads, HEAD_SIZE),
            value_rows[0].reshape(tok, kv_heads, HEAD_SIZE),
        ],
        axis=2,
    )
    cache_part = jnp.concatenate([cache_keys[0, 0], cache_values[0, 0]], axis=1)
    spread = jnp.broadcast_to(
        kv_rows[:, :, None, :], (tok, kv_heads, GROUP, 2 * HEAD_SIZE)
    ).reshape(tok, heads, 2 * HEAD_SIZE)
    mine = lax.all_to_all(
        jnp.concatenate([q_rows, spread], axis=2), "seq", split_axis=1, concat_axis=0, tiled=True
    )
    own_query = mine[:, 0, :HEAD_SIZE]
    stretch_kv = mine[:, 0, HEAD_SIZE:]
    cache_kv = assemble(cache_part, bits, rank)
    all_kv = jnp.concatenate([cache_kv, stretch_kv], axis=0)
    verts = vertical[0, 0]
    count = vertical_count[0, 0]
    slashes = slash[0, 0]
    tiles = (count + TILE - 1) // TILE
    start = (
        jnp.full((prefill_stretch,), big_negative, jnp.float32),
        jnp.zeros((prefill_stretch,), jnp.float32),
        jnp.zeros((prefill_stretch, HEAD_SIZE), jnp.float32),
    )
    carry = vertical_run(own_query, verts, count, 0, tiles, all_kv, start)
    top, total, accum = slash_run(own_query, verts, count, slashes, all_kv, carry)
    result = (accum / total[:, None]).astype(jnp.bfloat16)
    back = lax.all_to_all(
        result.reshape(prefill_stretch, 1, HEAD_SIZE),
        "seq",
        split_axis=0,
        concat_axis=1,
        tiled=True,
    )
    return back.reshape(1, tok, heads * HEAD_SIZE)


def solution(mesh):
    return jax.shard_map(
        per_device,
        mesh=mesh,
        in_specs=(
            P("section", "seq", None),
            P("section", "seq", None),
            P("section", "seq", None),
            P("section", "seq", None, None),
            P("section", "seq", None, None),
            P("section", "seq", None),
            P("section", "seq"),
            P("section", "seq", None),
        ),
        out_specs=P("section", "seq", None),
        check_vma=False,
    )
```

profile of v0, /device:TPU:0, one launch (start us, length us, event | category | flops | bytes accessed | tf_op | source)
XLA Modules:
  0.0 233.2 jit_solution(16334900830919298795)
XLA Ops:
  1.0 3.0 %collective-permute-start = (bf16[512,256]{1,0:T(8,128)(2,1)S(1)}, bf16[512,256]{1,0:T(8,128)(2,1)S(1)}, u32[]{:S(2)}, u32[]{:S(2)}) collective-permute-start(bf16[512,256]{1,0:T(8,128)(2,1)S(1)} %pad_maximum_fusion.5), channel_id=1, source_target_pairs={{0,1},{1,0},{2,3},{3,2},{4,5},{5,4},{6,7},{7,6},{8,9},{9,8},{10,11... | collective-permute-start | bytes 786440 | tf_op jit(solution)/shard_map/ppermute | solution.py:23
  7.2 3.2 %collective-permute-done = bf16[512,256]{1,0:T(8,128)(2,1)S(1)} collective-permute-done((bf16[512,256]{1,0:T(8,128)(2,1)S(1)}, bf16[512,256]{1,0:T(8,128)(2,1)S(1)}, u32[]{:S(2)}, u32[]{:S(2)}) %collective-permute-start) | collective-permute-done | bytes 262176 | tf_op jit(solution)/shard_map/ppermute | solution.py:23
  14.5 4.8 %all-to-all-start = ((bf16[128,8,384]{2,0,1:T(8,128)(2,1)}), bf16[128,8,384]{2,0,1:T(8,128)(2,1)S(1)}, u32[]{:S(2)}, u32[]{:S(2)}) async-start(bf16[128,8,384]{2,0,1:T(8,128)(2,1)} %pad_maximum_fusion.3), calls=%async_computation | async-start | bytes 1572864 | tf_op jit(solution)/shard_map/all_to_all | solution.py:173
  19.9 14.5 %collective-permute-done.1 = bf16[1024,256]{1,0:T(8,128)(2,1)S(1)} collective-permute-done((bf16[1024,256]{1,0:T(8,128)(2,1)S(1)}, bf16[1024,256]{1,0:T(8,128)(2,1)S(1)}, u32[]{:S(2)}, u32[]{:S(2)}) %collective-permute-start.1) | collective-permute-done | bytes 524320 | tf_op jit(solution)/shard_map/ppermute | solution.py:23
  35.6 3.3 %collective-permute-start.2 = (bf16[2048,256]{1,0:T(8,128)(2,1)}, bf16[2048,256]{1,0:T(8,128)(2,1)S(1)}, u32[]{:S(2)}, u32[]{:S(2)}) collective-permute-start(bf16[2048,256]{1,0:T(8,128)(2,1)} %pad_maximum_fusion.2), channel_id=1, source_target_pairs={{0,4},{1,5},{2,6},{3,7},{4,0},{5,1},{6,2},{7,3},{8,12},{9,13},{10,... | collective-permute-start | bytes 3145736 | tf_op jit(solution)/shard_map/ppermute | solution.py:23
  39.0 24.0 %all-to-all-done = bf16[128,8,384]{2,0,1:T(8,128)(2,1)S(1)} async-done(((bf16[128,8,384]{2,0,1:T(8,128)(2,1)}), bf16[128,8,384]{2,0,1:T(8,128)(2,1)S(1)}, u32[]{:S(2)}, u32[]{:S(2)}) %all-to-all-start) | async-done | bytes 786464 | tf_op jit(solution)/shard_map/all_to_all | solution.py:173
  63.7 19.5 %collective-permute-done.2 = bf16[2048,256]{1,0:T(8,128)(2,1)S(1)} collective-permute-done((bf16[2048,256]{1,0:T(8,128)(2,1)}, bf16[2048,256]{1,0:T(8,128)(2,1)S(1)}, u32[]{:S(2)}, u32[]{:S(2)}) %collective-permute-start.2) | collective-permute-done | bytes 1048608 | tf_op jit(solution)/shard_map/ppermute | solution.py:23
  83.8 10.0 %pad_maximum_fusion = bf16[6144,256]{1,0:T(8,128)(2,1)} fusion(bf16[1024,256]{1,0:T(8,128)(2,1)S(1)} %slice_bitcast_fusion, bf16[2048,256]{1,0:T(8,128)(2,1)S(1)} %get-tuple-element.252, bf16[2048,256]{1,0:T(8,128)(2,1)S(1)} %get-tuple-element.251, bf16[6144]{0:T(1024)(128)(2,1)S(1)} %pad.3.clone), kind=kLoop, calls=%fused_computation.59 | loop fusion | flops 12582912 | bytes 5779456 | tf_op jit(solution)/shard_map/concatenate | solution.py:85
  94.7 18.5 %while.31 = (s32[]{:T(128)}, f32[1024]{0:T(1024)S(1)}, f32[1024]{0:T(1024)S(1)}, f32[1024,128]{1,0:T(8,128)}, s32[]{:T(128)}, /*index=5*/s32[]{:T(128)}, s32[32]...) while((s32[]{:T(128)}, f32[1024]{0:T(1024)S(1)}, ...), condition=%wide.region_4.5_spmd.clone, body=%wide.region_1.4_spmd.clone.sunk | while | flops 136907808 | bytes 5184775 | solution.py:66
  97.0 2.3 convolution_add_fusion.2
  101.6 2.3 convolution_add_fusion.2
  106.2 2.3 convolution_add_fusion.2
  110.8 2.3 convolution_add_fusion.2
  113.3 82.7 %while.33 = (s32[]{:T(128)}, f32[2,8,64]{2,1,0:T(8,128)S(1)}, f32[2,8,64,128]{3,2,1,0:T(8,128)}, f32[2,8,64]{2,1,0:T(8,128)S(1)}, f32[2,8,64]{2,1,0:T(8,128)S(1)...) while((s32[]{:T(128)}, f32[2,8,64]{2,1,0:T(8,128)S(1)}, ...), condition=%wide.region_8.9_spmd.clone, body=%wide.region_5.8_spmd.clone.sunk | while | flops 206276656 | bytes 19812000 | solution.py:135
  114.6 34.3 %while.34 = (s32[]{:T(128)}, bf16[6144,256]{1,0:T(8,128)(2,1)}, s32[12,2]{0,1:T(2,128)S(1)}, bf16[12,512,256]{2,1,0:T(8,128)(2,1)}, s32[]{:T(128)}) while((s32[]{:T(128)}, bf16[6144,256]{1,0:T(8,128)(2,1)}, s32[12,2]{0,1:T(2,128)S(1)}, bf16[12,512,256]{2,1,0:T(8,128)(2,1)}, s32[]{:T(128)}) %tuple.74), condition=%wide.while_cond, body=%wide.while_body.sunk | while | flops 2 | bytes 525401 | solution.py:96
  129.4 2.3 bitcast_dynamic-update-slice_fusion.2
  132.3 2.3 bitcast_dynamic-update-slice_fusion.2
  138.0 2.3 bitcast_dynamic-update-slice_fusion.2
  155.9 34.3 %while.34 = (s32[]{:T(128)}, bf16[6144,256]{1,0:T(8,128)(2,1)}, s32[12,2]{0,1:T(2,128)S(1)}, bf16[12,512,256]{2,1,0:T(8,128)(2,1)}, s32[]{:T(128)}) while((s32[]{:T(128)}, bf16[6144,256]{1,0:T(8,128)(2,1)}, s32[12,2]{0,1:T(2,128)S(1)}, bf16[12,512,256]{2,1,0:T(8,128)(2,1)}, s32[]{:T(128)}) %tuple.74), condition=%wide.while_cond, body=%wide.while_body.sunk | while | flops 2 | bytes 525401 | solution.py:96
  170.8 2.3 bitcast_dynamic-update-slice_fusion.2
  173.6 2.3 bitcast_dynamic-update-slice_fusion.2
  179.4 2.3 bitcast_dynamic-update-slice_fusion.2
  196.1 3.9 %divide_convert_fusion = bf16[1024,1,128]{2,1,0:T(2,128)(2,1)S(1)} fusion(f32[1024,1,128]{2,1,0:T(1,128)} %bitcast.110, f32[1024]{0:T(1024)S(1)} %div.49), kind=kLoop, calls=%fused_computation.67 | loop fusion | flops 262144 | bytes 790528 | tf_op jit(solution)/shard_map/convert_element_type | solution.py:191
  202.8 29.1 %all_to_all.33 = bf16[8,2,8192]{2,1,0:T(2,128)(2,1)S(1)} all-to-all(bf16[8,2,8192]{2,1,0:T(2,128)(2,1)S(1)} %reshape.230), channel_id=1, replica_groups=mesh['section'=4,'seq'=8] {'seq'}, dimensions={0} | all-to-all | bytes 524288 | tf_op jit(solution)/shard_map/all_to_all | solution.py:192
  (208 shorter events, 92.4 us)
Async XLA Ops:
  1.0 9.3 %collective-permute-start = (bf16[512,256]{1,0:T(8,128)(2,1)S(1)}, bf16[512,256]{1,0:T(8,128)(2,1)S(1)}, u32[]{:S(2)}, u32[]{:S(2)}) collective-permute-start(bf16[512,256]{1,0:T(8,128)(2,1)S(1)} %pad_maximum_fusion.5), channel_id=1, source_target_pairs={{0,1},{1,0},{2,3},{3,2},{4,5},{5,4},{6,7},{7,6},{8,9},{9,8},{10,11... | collective-permute-start | bytes 786440 | tf_op jit(solution)/shard_map/ppermute | solution.py:23
  4.0 9.4 %collective-permute-start.3 = (bf16[1,128,1024]{2,1,0:T(8,128)(2,1)}, bf16[1,128,1024]{2,1,0:T(8,128)(2,1)S(1)}, u32[]{:S(2)}, u32[]{:S(2)}) collective-permute-start(bf16[1,128,1024]{2,1,0:T(8,128)(2,1)} %param.12), channel_id=1, source_target_pairs={{0,8},{8,16},{16,24},{24,0},{1,9},{9,17},{17,25},{25,1},{2,10},{10... | collective-permute-start | bytes 786440 | tf_op jit(solution)/shard_map/ppermute | solution.py:28
  4.0 9.3 %collective-permute-start.4 = (bf16[1,128,128]{2,1,0:T(8,128)(2,1)}, bf16[1,128,128]{2,1,0:T(8,128)(2,1)S(1)}, u32[]{:S(2)}, u32[]{:S(2)}) collective-permute-start(bf16[1,128,128]{2,1,0:T(8,128)(2,1)} %param.13), channel_id=1, source_target_pairs={{0,8},{8,16},{16,24},{24,0},{1,9},{9,17},{17,25},{25,1},{2,10},{10... | collective-permute-start | bytes 98312 | tf_op jit(solution)/shard_map/ppermute | solution.py:28
  5.6 7.7 %collective-permute-start.5 = (bf16[1,128,128]{2,1,0:T(8,128)(2,1)}, bf16[1,128,128]{2,1,0:T(8,128)(2,1)S(1)}, u32[]{:S(2)}, u32[]{:S(2)}) collective-permute-start(bf16[1,128,128]{2,1,0:T(8,128)(2,1)} %param.14), channel_id=1, source_target_pairs={{0,8},{8,16},{16,24},{24,0},{1,9},{9,17},{17,25},{25,1},{2,10},{10... | collective-permute-start | bytes 98312 | tf_op jit(solution)/shard_map/ppermute | solution.py:28
  11.4 8.0 %copy-start.3 = (s32[1,1,32]{2,1,0:T(1,128)S(1)}, s32[1,1,32]{2,1,0:T(1,128)}, u32[]{:S(2)}) copy-start(s32[1,1,32]{2,1,0:T(1,128)} %param.17) | copy-start | bytes 388
  11.4 22.9 %collective-permute-start.1 = (bf16[1024,256]{1,0:T(8,128)(2,1)S(1)}, bf16[1024,256]{1,0:T(8,128)(2,1)S(1)}, u32[]{:S(2)}, u32[]{:S(2)}) collective-permute-start(bf16[1024,256]{1,0:T(8,128)(2,1)S(1)} %pad_maximum_fusion.4), channel_id=1, source_target_pairs={{0,2},{1,3},{2,0},{3,1},{4,6},{5,7},{6,4},{7,5},{8,10},{9,11},{10,... | collective-permute-start | bytes 1572872 | tf_op jit(solution)/shard_map/ppermute | solution.py:23
  14.5 48.4 %all-to-all-start = ((bf16[128,8,384]{2,0,1:T(8,128)(2,1)}), bf16[128,8,384]{2,0,1:T(8,128)(2,1)S(1)}, u32[]{:S(2)}, u32[]{:S(2)}) async-start(bf16[128,8,384]{2,0,1:T(8,128)(2,1)} %pad_maximum_fusion.3), calls=%async_computation | async-start | bytes 1572864 | tf_op jit(solution)/shard_map/all_to_all | solution.py:173
  35.6 47.7 %collective-permute-start.2 = (bf16[2048,256]{1,0:T(8,128)(2,1)}, bf16[2048,256]{1,0:T(8,128)(2,1)S(1)}, u32[]{:S(2)}, u32[]{:S(2)}) collective-permute-start(bf16[2048,256]{1,0:T(8,128)(2,1)} %pad_maximum_fusion.2), channel_id=1, source_target_pairs={{0,4},{1,5},{2,6},{3,7},{4,0},{5,1},{6,2},{7,3},{8,12},{9,13},{10,... | collective-permute-start | bytes 3145736 | tf_op jit(solution)/shard_map/ppermute | solution.py:23
  94.7 18.6 %copy-start.2 = (bf16[1024,1,128]{2,0,1:T(8,128)(2,1)S(1)}, bf16[1024,1,128]{2,0,1:T(8,128)(2,1)}, u32[]{:S(2)}) copy-start(bf16[1024,1,128]{2,0,1:T(8,128)(2,1)} %get-tuple-element.255) | copy-start | bytes 786436
  151.2 1.0 copy-start
  153.8 0.8 copy-start.1
  192.5 1.0 copy-start
  195.2 0.8 copy-start.1
where the time goes:
time: 236 us; the launch traced here: 233 us
  local copies, waits for them, and re-layouts  82.7 us (35%)
  waiting for transfers between devices  61.1 us (26%)
  blocking collectives  29.1 us (12%)
  other arithmetic  27.8 us (12%)
  matrix products  15.2 us (6%)
  starting transfers between devices  14.7 us (6%)
    gather x72, local copies, waits for them, and re-layouts  68.5 us
    ppermute x3, waiting for transfers between devices, from_partner(): return lax.ppermute(value, axis, pairs)  37.1 us
    all_to_all x1, blocking collectives, per_device(): lax.all_to_all(result.reshape(prefill_stretch, 1, HEAD_SIZE), 'seq', spli...  29.1 us
    all_to_all x1, waiting for transfers between devices, per_device(): lax.all_to_all(jnp.concatenate([q_rows, spread], axis=2), 'seq', split_ax...  24 us
    concatenate x1, other arithmetic, slash_run(): jnp.concatenate([jnp.zeros((prefill_stretch, 2 * HEAD_SIZE), all_kv.dtype...  10 us
    dot_general x4, matrix products, contract(): jnp.dot(attention_weight, value_tile, preferred_element_type=jnp.float32)  9.24 us
    ppermute x3, starting transfers between devices, from_partner(): return lax.ppermute(value, axis, pairs)  8.2 us
    convert_element_type x2, other arithmetic, per_device(): result = (accum / total[:, None]).astype(jnp.bfloat16)  6.1 us
  transfers between devices with their start and end apart: 7, of which 4 were waited for; matrix products, arithmetic and copies ran while one was open for 2% of the time, Pallas kernels for 0%

commit v1 on v0

v1 whole, which is shorter than its diff:
```python
import functools
import math

import jax
import jax.numpy as jnp
from jax import lax
from jax.experimental import pallas as pl
from jax.experimental.pallas import tpu as pltpu
from jax.sharding import PartitionSpec as P

HEAD = 128
GROUP = 8
BLK = 64
NVMAX = 32
NS = 11
LANES = 128
MASKED = -1e30
MESH = pl.DeviceIdType.MESH
UP, DOWN, ACROSS = 0, 1, 2
CK, CV, SK, SV = 0, 1, 2, 3


def kernel(
    layers,
    n,
    q_hbm,
    k_hbm,
    v_hbm,
    ck_hbm,
    cv_hbm,
    vert_ref,
    count_ref,
    slash_ref,
    out_ref,
    ckbuf,
    cvbuf,
    skbuf,
    svbuf,
    qbuf,
    tabs,
    tabr,
    qaug,
    acc,
    top,
    local_sem,
    shift_send,
    q_recv,
    send_sem,
    recv_sem,
    tab_send,
    tab_recv,
):
    tok = qbuf.shape[0]
    part = ckbuf.shape[1]
    kvh = skbuf.shape[2] // HEAD
    per = tok // BLK
    ncb = GROUP * part // BLK
    nqb = n * per
    rows_of_group = GROUP * tok
    tile = min(2 * tok, rows_of_group)
    outer = n // 2
    sec = lax.axis_index("section")
    me = lax.axis_index("seq")
    o, i = me // 2, me % 2
    after, before = lax.rem(sec + 1, layers), lax.rem(sec + layers - 1, layers)
    scale = math.log2(math.e) / math.sqrt(HEAD)

    barrier = pltpu.get_barrier_semaphore()
    for d in range(1, n):
        pl.semaphore_signal(
            barrier, inc=1, device_id={"seq": lax.rem(me + d, n)}, device_id_type=MESH
        )
    for other in (after, before):
        pl.semaphore_signal(barrier, inc=1, device_id={"section": other}, device_id_type=MESH)
    pl.semaphore_wait(barrier, n + 1)

    bufs = (ckbuf, cvbuf, skbuf, svbuf)
    target = (me + 2, me - 2, me + 1 - 2 * i)

    def relay(which, slot, way, src=None):
        dst = bufs[which].at[slot]
        return pltpu.make_async_remote_copy(
            src_ref=dst if src is None else src,
            dst_ref=dst,
            send_sem=send_sem.at[way, which, slot],
            recv_sem=recv_sem.at[which, slot],
            device_id={"seq": target[way]},
            device_id_type=MESH,
        )

    def shift(src, dst, index, recv):
        return pltpu.make_async_remote_copy(
            src_ref=src,
            dst_ref=dst,
            send_sem=shift_send.at[index],
            recv_sem=recv,
            device_id={"section": after},
            device_id_type=MESH,
        )

    shifts = (
        shift(k_hbm, skbuf.at[me], 0, recv_sem.at[SK, me]),
        shift(v_hbm, svbuf.at[me], 1, recv_sem.at[SV, me]),
        shift(q_hbm, qbuf, 2, q_recv),
    )
    for copy in shifts:
        copy.start()
    own = ((CK, ck_hbm), (CV, cv_hbm))
    for which, src in own:
        relay(which, me, ACROSS, src).start()

        @pl.when(o < outer - 1)
        def _():
            relay(which, me, UP, src).start()

        @pl.when(o > 0)
        def _():
            relay(which, me, DOWN, src).start()

    locals_ = [
        pltpu.make_async_copy(src, bufs[which].at[me], local_sem.at[which]) for which, src in own
    ]
    for copy in locals_:
        copy.start()

    lane = lax.broadcasted_iota(jnp.int32, (1, LANES), 1)
    count = count_ref[0, 0]
    hit = lane < 0
    for slot in range(NVMAX):
        hit = hit | (lane == jnp.where(slot < count, vert_ref[0, slot], -1))
    listed = jnp.where(hit, 1, 0)
    offsets = [slash_ref[0, j] for j in range(NS)]

    def fill(b, carry):
        diagonal = ncb + b
        found = (listed > 0) | (lane == diagonal)
        for off in offsets:
            found = found | (lane == diagonal - off)
        tabs[b] = jnp.where(found, 0.0, MASKED)
        return carry

    lax.fori_loop(0, nqb, fill, 0)

    def table(d):
        to = lax.rem(me + d, n)
        return pltpu.make_async_remote_copy(
            src_ref=tabs.at[pl.ds(to * per, per)],
            dst_ref=tabr.at[me],
            send_sem=tab_send.at[d],
            recv_sem=tab_recv.at[me],
            device_id={"seq": to},
            device_id_type=MESH,
        )

    for d in range(1, n):
        table(d).start()
    tabr[me] = tabs[pl.ds(me * per, per)]

    for which in (SK, SV):
        relay(which, me, UP).wait_recv()

        @pl.when(o < outer - 1)
        def _():
            relay(which, me, UP).start()

        @pl.when(i == 0)
        def _():
            relay(which, me, ACROSS).start()

    shifts[2].wait_recv()
    for d in range(1, n):
        src = lax.rem(me + d, n)
        pltpu.make_async_remote_copy(
            src_ref=tabs.at[pl.ds(0, per)],
            dst_ref=tabr.at[src],
            send_sem=tab_send.at[d],
            recv_sem=tab_recv.at[src],
            device_id={"seq": src},
            device_id_type=MESH,
        ).wait_recv()
    for h in range(n):
        qaug[h * tok : (h + 1) * tok, :HEAD] = qbuf[:, h * HEAD : (h + 1) * HEAD]
        for j in range(per):
            qaug[h * tok + j * BLK : h * tok + (j + 1) * BLK, HEAD:] = jnp.broadcast_to(
                tabr[h, j].astype(jnp.bfloat16), (BLK, LANES)
            )

    def attend(keys, values, first_block, base, diagonal=False):
        width = keys.shape[0]
        block = lax.broadcasted_iota(jnp.int32, (width, LANES), 0) // BLK + first_block
        mark = lax.broadcasted_iota(jnp.int32, (width, LANES), 1) == block
        keys = jnp.concatenate([keys, jnp.where(mark, 1.0, 0.0).astype(jnp.bfloat16)], axis=1)
        values = jnp.concatenate([values, jnp.ones((width, LANES), jnp.bfloat16)], axis=1)
        span = width // LANES

        def body(step, carry):
            rows = pl.ds(pl.multiple_of(base + step * tile, tile), tile)
            scores = lax.dot_general(
                qaug[rows, :], keys, (((1,), (1,)), ((), ())), preferred_element_type=jnp.float32
            )
            if diagonal:
                token = lax.rem(lax.broadcasted_iota(jnp.int32, (tile, width), 0), tok)
                key = lax.broadcasted_iota(jnp.int32, (tile, width), 1)
                scores = jnp.where(key <= token, scores, MASKED)
            high = jnp.broadcast_to(jnp.max(scores, axis=1, keepdims=True), (tile, LANES))
            if not diagonal:
                old = top[rows, :]
                high = jnp.maximum(old, high)
            top[rows, :] = high
            wide = jnp.concatenate([high] * span, axis=1)
            weights = jnp.exp2((scores - wide) * scale).astype(jnp.bfloat16)
            fresh = jnp.dot(weights, values, preferred_element_type=jnp.float32)
            if diagonal:
                acc[rows, :] = fresh
            else:
                factor = jnp.exp2((old - high) * scale)
                acc[rows, :] = acc[rows, :] * jnp.concatenate([factor] * 2, axis=1) + fresh
            return carry

        lax.fori_loop(0, rows_of_group // tile, body, 0)

    def attend_cache(slot):
        attend(
            ckbuf[slot],
            cvbuf[slot],
            lax.rem(slot, GROUP) * (part // BLK),
            slot // GROUP * rows_of_group,
        )

    def attend_stretch(slot, slots, diagonal=False):
        for g in range(kvh):
            keys = skbuf[pl.ds(slot, slots), :, g * HEAD : (g + 1) * HEAD]
            values = svbuf[pl.ds(slot, slots), :, g * HEAD : (g + 1) * HEAD]
            attend(
                keys.reshape(slots * tok, HEAD),
                values.reshape(slots * tok, HEAD),
                ncb + slot * per,
                g * rows_of_group,
                diagonal,
            )

    attend_stretch(me, 1, diagonal=True)
    for copy in locals_:
        copy.wait()
    attend_cache(me)

    def across(k):
        low, high = me - 2 * k + 1 - 2 * i, me + 2 * k + 1 - 2 * i

        @pl.when(o - k >= 0)
        def _():
            for which in (CK, CV, SK, SV):
                relay(which, low, ACROSS).wait_recv()
            attend_cache(low)
            attend_stretch((o - k) * 2, 2)

        @pl.when(o + k < outer)
        def _():
            for which in (CK, CV):
                relay(which, high, ACROSS).wait_recv()
            attend_cache(high)

    def step(k, carry):
        low, high = me - 2 * k, me + 2 * k

        @pl.when(o - k >= 0)
        def _():
            for which in (CK, CV, SK, SV):
                relay(which, low, UP).wait_recv()

                @pl.when(o < outer - 1)
                def _():
                    relay(which, low, UP).start()

                relay(which, low, ACROSS).start()

        @pl.when(o + k < outer)
        def _():
            for which in (CK, CV):
                relay(which, high, DOWN).wait_recv()

                @pl.when(o > 0)
                def _():
                    relay(which, high, DOWN).start()

                relay(which, high, ACROSS).start()

        @pl.when(k > 1)
        def _():
            across(k - 1)

        @pl.when(k == 1)
        def _():
            partner = me + 1 - 2 * i
            for which in (CK, CV):
                relay(which, partner, ACROSS).wait_recv()
            attend_cache(partner)

            @pl.when(i == 1)
            def _():
                for which in (SK, SV):
                    relay(which, partner, ACROSS).wait_recv()
                attend_stretch(partner, 1)

        @pl.when(o - k >= 0)
        def _():
            attend_cache(low)

        @pl.when(o + k < outer)
        def _():
            attend_cache(high)

        return carry

    lax.fori_loop(1, outer, step, 0)
    across(outer - 1)

    for h in range(n):
        rows = slice(h * tok, (h + 1) * tok)
        out_ref[:, h * HEAD : (h + 1) * HEAD] = (acc[rows, :HEAD] / acc[rows, HEAD:]).astype(
            out_ref.dtype
        )

    for copy in shifts:
        copy.wait_send()
    for d in range(1, n):
        table(d).wait_send()
    for which, src in own:
        relay(which, me, ACROSS, src).wait_send()

        @pl.when(o < outer - 1)
        def _():
            relay(which, me, UP, src).wait_send()

        @pl.when(o > 0)
        def _():
            relay(which, me, DOWN, src).wait_send()

    for which in (SK, SV):

        @pl.when(o < outer - 1)
        def _():
            relay(which, me, UP).wait_send()

        @pl.when(i == 0)
        def _():
            relay(which, me, ACROSS).wait_send()

    def drain(k, carry):
        low, high = me - 2 * k, me + 2 * k

        @pl.when(o - k >= 0)
        def _():
            for which in (CK, CV, SK, SV):

                @pl.when(o < outer - 1)
                def _():
                    relay(which, low, UP).wait_send()

                relay(which, low, ACROSS).wait_send()

        @pl.when(o + k < outer)
        def _():
            for which in (CK, CV):

                @pl.when(o > 0)
                def _():
                    relay(which, high, DOWN).wait_send()

                relay(which, high, ACROSS).wait_send()

        return carry

    lax.fori_loop(1, outer, drain, 0)


def solution(mesh):
    layers, n = mesh.shape["section"], mesh.shape["seq"]

    def per_device(queries, keys, values, cache_keys, cache_values, vertical, count, slash):
        tok, wide = queries.shape[1:]
        kv_wide = keys.shape[2]
        part = cache_keys.shape[2]
        per = tok // BLK
        dtype = queries.dtype
        rows = n * tok
        anywhere = pl.BlockSpec(memory_space=pl.ANY)
        scalars = pl.BlockSpec(memory_space=pltpu.SMEM)
        keys_all = GROUP * part + n * tok
        result = pl.pallas_call(
            functools.partial(kernel, layers, n),
            out_shape=jax.ShapeDtypeStruct((tok, wide), dtype),
            in_specs=[anywhere] * 5 + [scalars] * 3,
            out_specs=pl.BlockSpec(memory_space=pltpu.VMEM),
            scratch_shapes=[
                pltpu.VMEM((n, part, HEAD), dtype),
                pltpu.VMEM((n, part, HEAD), dtype),
                pltpu.VMEM((n, tok, kv_wide), dtype),
                pltpu.VMEM((n, tok, kv_wide), dtype),
                pltpu.VMEM((tok, wide), dtype),
                pltpu.VMEM((n * per, 1, LANES), jnp.float32),
                pltpu.VMEM((n, per, 1, LANES), jnp.float32),
                pltpu.VMEM((rows, 2 * HEAD), dtype),
                pltpu.VMEM((rows, 2 * HEAD), jnp.float32),
                pltpu.VMEM((rows, LANES), jnp.float32),
                pltpu.SemaphoreType.DMA((2,)),
                pltpu.SemaphoreType.DMA((3,)),
                pltpu.SemaphoreType.DMA,
                pltpu.SemaphoreType.DMA((3, 4, n)),
                pltpu.SemaphoreType.DMA((4, n)),
                pltpu.SemaphoreType.DMA((n,)),
                pltpu.SemaphoreType.DMA((n,)),
            ],
            compiler_params=pltpu.CompilerParams(
                collective_id=0, has_side_effects=True, vmem_limit_bytes=50 * 2**20
            ),
            cost_estimate=pl.CostEstimate(
                flops=4 * rows * keys_all * HEAD,
                bytes_accessed=2 * rows * HEAD * 4,
                transcendentals=rows * keys_all,
            ),
        )(
            queries[0],
            keys[0],
            values[0],
            cache_keys[0, 0],
            cache_values[0, 0],
            vertical[0],
            count,
            slash[0],
        )
        return result[None]

    return jax.shard_map(
        per_device,
        mesh=mesh,
        in_specs=(
            P("section", "seq", None),
            P("section", "seq", None),
            P("section", "seq", None),
            P("section", "seq", None, None),
            P("section", "seq", None, None),
            P("section", "seq", None),
            P("section", "seq"),
            P("section", "seq", None),
        ),
        out_specs=P("section", "seq", None),
        check_vma=False,
    )
```

time: 236 us -> 51.1 us (0.22)
  the two profiles are of different devices: /device:TPU:0 before, /device:TPU:26 now
where the time goes in v1:
time: 51.1 us; the launch traced here: 50.7 us
  Pallas kernels  44.4 us (87%)
  local copies, waits for them, and re-layouts  5.63 us (11%)
  between operations  0.68 us (1%)
    pallas_call x1, Pallas kernels, per_device(): pl.pallas_call(functools.partial(kernel, layers, n), out_shape=jax.ShapeD...  44.4 us
    unnamed x15, local copies, waits for them, and re-layouts  5.63 us

profile of v1, /device:TPU:26, one launch (start us, length us, event | category | flops | bytes accessed | tf_op | source)
XLA Modules:
  0.0 50.7 jit_solution(9526346024664019339)
XLA Ops:
  0.7 0.0 copy-start.5
  0.7 0.0 copy-start.6
  0.7 0.6 %copy-done.5 = s32[1,1,32]{2,1,0:T(1,128)S(1)} copy-done((s32[1,1,32]{2,1,0:T(1,128)S(1)}, s32[1,1,32]{2,1,0:T(1,128)}, u32[]{:S(2)}) %copy-start.5) | copy-done | bytes 152
  1.3 0.0 copy-done.6
  1.3 0.0 copy-start
  1.3 0.9 %copy-done = bf16[1,128,1024]{2,1,0:T(8,128)(2,1)S(1)} copy-done((bf16[1,128,1024]{2,1,0:T(8,128)(2,1)S(1)}, bf16[1,128,1024]{2,1,0:T(8,128)(2,1)}, u32[]{:S(2)}) %copy-start) | copy-done | bytes 262168
  2.3 0.0 copy-start.1
  2.3 0.9 %copy-done.1 = bf16[1,1,512,128]{3,2,1,0:T(8,128)(2,1)S(1)} copy-done((bf16[1,1,512,128]{3,2,1,0:T(8,128)(2,1)S(1)}, bf16[1,1,512,128]{3,2,1,0:T(8,128)(2,1)}, u32[]{:S(2)}) %copy-start.1) | copy-done | bytes 131096
  3.2 0.0 copy-start.2
  3.2 0.9 %copy-done.2 = bf16[1,1,512,128]{3,2,1,0:T(8,128)(2,1)S(1)} copy-done((bf16[1,1,512,128]{3,2,1,0:T(8,128)(2,1)S(1)}, bf16[1,1,512,128]{3,2,1,0:T(8,128)(2,1)}, u32[]{:S(2)}) %copy-start.2) | copy-done | bytes 131096
  4.1 0.0 copy-start.3
  4.1 0.8 %copy-done.3 = bf16[1,128,128]{2,1,0:T(8,128)(2,1)S(1)} copy-done((bf16[1,128,128]{2,1,0:T(8,128)(2,1)S(1)}, bf16[1,128,128]{2,1,0:T(8,128)(2,1)}, u32[]{:S(2)}) %copy-start.3) | copy-done | bytes 32792
  4.8 0.0 copy-start.4
  4.8 0.8 %copy-done.4 = bf16[1,128,128]{2,1,0:T(8,128)(2,1)S(1)} copy-done((bf16[1,128,128]{2,1,0:T(8,128)(2,1)S(1)}, bf16[1,128,128]{2,1,0:T(8,128)(2,1)}, u32[]{:S(2)}) %copy-start.4) | copy-done | bytes 32792
  5.6 44.4 %shard_map.82 = bf16[128,1024]{1,0:T(8,128)(2,1)S(1)} custom-call(bf16[128,1024]{1,0:T(8,128)(2,1)S(1)} %bitcast.9, bf16[128,128]{1,0:T(8,128)(2,1)S(1)} %bitcast.12, bf16[128,128]{1,0:T(8,128)(2,1)S(1)} %bitcast.13, bf16[512,128]{1,0:T(8,128)(2,1)S(1)} %bitcast.10, bf16[512,128]{1,0:T(8,128)(2,1)S(1)} %bitcast.11, s32[1,32]{1,0:T(1,128)S(1)} %bitcast.14, ...), custom_call_target="tpu_custom_call" | custom-call | flops 2684354560 | bytes 1048576 | tf_op jit(solution)/shard_map/pallas_call | solution.py:390
  50.0 0.7 %copy.11 = bf16[1,128,1024]{2,1,0:T(8,128)(2,1)} copy(bf16[1,128,1024]{2,1,0:T(8,128)(2,1)S(1)} %bitcast.8) | data formatting | bytes 524288
Async XLA Ops:
  0.7 0.7 %copy-start.5 = (s32[1,1,32]{2,1,0:T(1,128)S(1)}, s32[1,1,32]{2,1,0:T(1,128)}, u32[]{:S(2)}) copy-start(s32[1,1,32]{2,1,0:T(1,128)} %param.13) | copy-start | bytes 388
  0.7 0.7 %copy-start.6 = (s32[1,1,11]{2,1,0:T(1,128)S(1)}, s32[1,1,11]{2,1,0:T(1,128)}, u32[]{:S(2)}) copy-start(s32[1,1,11]{2,1,0:T(1,128)} %param.15) | copy-start | bytes 136
  1.3 0.9 %copy-start = (bf16[1,128,1024]{2,1,0:T(8,128)(2,1)S(1)}, bf16[1,128,1024]{2,1,0:T(8,128)(2,1)}, u32[]{:S(2)}) copy-start(bf16[1,128,1024]{2,1,0:T(8,128)(2,1)} %param.8) | copy-start | bytes 786436
  2.3 0.9 %copy-start.1 = (bf16[1,1,512,128]{3,2,1,0:T(8,128)(2,1)S(1)}, bf16[1,1,512,128]{3,2,1,0:T(8,128)(2,1)}, u32[]{:S(2)}) copy-start(bf16[1,1,512,128]{3,2,1,0:T(8,128)(2,1)} %param.11) | copy-start | bytes 393220
  3.2 0.9 %copy-start.2 = (bf16[1,1,512,128]{3,2,1,0:T(8,128)(2,1)S(1)}, bf16[1,1,512,128]{3,2,1,0:T(8,128)(2,1)}, u32[]{:S(2)}) copy-start(bf16[1,1,512,128]{3,2,1,0:T(8,128)(2,1)} %param.12) | copy-start | bytes 393220
  4.1 0.8 %copy-start.3 = (bf16[1,128,128]{2,1,0:T(8,128)(2,1)S(1)}, bf16[1,128,128]{2,1,0:T(8,128)(2,1)}, u32[]{:S(2)}) copy-start(bf16[1,128,128]{2,1,0:T(8,128)(2,1)} %param.9) | copy-start | bytes 98308
  4.8 0.8 %copy-start.4 = (bf16[1,128,128]{2,1,0:T(8,128)(2,1)S(1)}, bf16[1,128,128]{2,1,0:T(8,128)(2,1)}, u32[]{:S(2)}) copy-start(bf16[1,128,128]{2,1,0:T(8,128)(2,1)} %param.10) | copy-start | bytes 98308

commit v2 on v1

--- a/solution.py
+++ b/solution.py
@@ -193,8 +193,7 @@
         values = jnp.concatenate([values, jnp.ones((width, LANES), jnp.bfloat16)], axis=1)
         span = width // LANES
 
-        def body(step, carry):
-            rows = pl.ds(pl.multiple_of(base + step * tile, tile), tile)
+        def scores_of(rows):
             scores = lax.dot_general(
                 qaug[rows, :], keys, (((1,), (1,)), ((), ())), preferred_element_type=jnp.float32
             )
@@ -202,6 +201,9 @@
                 token = lax.rem(lax.broadcasted_iota(jnp.int32, (tile, width), 0), tok)
                 key = lax.broadcasted_iota(jnp.int32, (tile, width), 1)
                 scores = jnp.where(key <= token, scores, MASKED)
+            return scores
+
+        def update(rows, scores):
             high = jnp.broadcast_to(jnp.max(scores, axis=1, keepdims=True), (tile, LANES))
             if not diagonal:
                 old = top[rows, :]
@@ -215,16 +217,24 @@
             else:
                 factor = jnp.exp2((old - high) * scale)
                 acc[rows, :] = acc[rows, :] * jnp.concatenate([factor] * 2, axis=1) + fresh
-            return carry
-
-        lax.fori_loop(0, rows_of_group // tile, body, 0)
+
+        spans = [
+            pl.ds(base + t * tile if kvh == 1 else pl.multiple_of(base + t * tile, tile), tile)
+            for t in range(rows_of_group // tile)
+        ]
+        ahead = scores_of(spans[0])
+        for t, rows in enumerate(spans):
+            scores = ahead
+            if t + 1 < len(spans):
+                ahead = scores_of(spans[t + 1])
+            update(rows, scores)
 
     def attend_cache(slot):
         attend(
             ckbuf[slot],
             cvbuf[slot],
             lax.rem(slot, GROUP) * (part // BLK),
-            slot // GROUP * rows_of_group,
+            0 if kvh == 1 else slot // GROUP * rows_of_group,
         )
 
     def attend_stretch(slot, slots, diagonal=False):
@@ -263,27 +273,35 @@
     def step(k, carry):
         low, high = me - 2 * k, me + 2 * k
 
-        @pl.when(o - k >= 0)
-        def _():
-            for which in (CK, CV, SK, SV):
-                relay(which, low, UP).wait_recv()
-
-                @pl.when(o < outer - 1)
-                def _():
-                    relay(which, low, UP).start()
-
-                relay(which, low, ACROSS).start()
-
-        @pl.when(o + k < outer)
-        def _():
-            for which in (CK, CV):
-                relay(which, high, DOWN).wait_recv()
-
-                @pl.when(o > 0)
-                def _():
-                    relay(which, high, DOWN).start()
-
-                relay(which, high, ACROSS).start()
+        def pass_up(*arrays):
+            @pl.when(o - k >= 0)
+            def _():
+                for which in arrays:
+                    relay(which, low, UP).wait_recv()
+
+                    @pl.when(o < outer - 1)
+                    def _():
+                        relay(which, low, UP).start()
+
+                    relay(which, low, ACROSS).start()
+
+        def pass_down(*arrays):
+            @pl.when(o + k < outer)
+            def _():
+                for which in arrays:
+                    relay(which, high, DOWN).wait_recv()
+
+                    @pl.when(o > 0)
+                    def _():
+                        relay(which, high, DOWN).start()
+
+                    relay(which, high, ACROSS).start()
+
+        pass_up(CK)
+        pass_down(CK)
+        pass_up(CV)
+        pass_down(CV)
+        pass_up(SK, SV)
 
         @pl.when(k > 1)
         def _():
@@ -384,7 +402,7 @@
         per = tok // BLK
         dtype = queries.dtype
         rows = n * tok
-        anywhere = pl.BlockSpec(memory_space=pl.ANY)
+        anywhere = pl.BlockSpec(memory_space=pltpu.HBM)
         scalars = pl.BlockSpec(memory_space=pltpu.SMEM)
         keys_all = GROUP * part + n * tok
         result = pl.pallas_call(
@@ -412,7 +430,7 @@
                 pltpu.SemaphoreType.DMA((n,)),
             ],
             compiler_params=pltpu.CompilerParams(
-                collective_id=0, has_side_effects=True, vmem_limit_bytes=50 * 2**20
+                collective_id=0, has_side_effects=True, vmem_limit_bytes=63 * 2**20
             ),
             cost_estimate=pl.CostEstimate(
                 flops=4 * rows * keys_all * HEAD,

time: 51.1 us -> 41.6 us (0.81)
  the two profiles are of different devices: /device:TPU:26 before, /device:TPU:24 now
where the time goes in v2:
time: 41.6 us; the launch traced here: 41.5 us
  Pallas kernels  39.1 us (94%)
  local copies, waits for them, and re-layouts  1.67 us (4%)
  between operations  0.66 us (2%)
    pallas_call x1, Pallas kernels, per_device(): pl.pallas_call(functools.partial(kernel, layers, n), out_shape=jax.ShapeD...  39.1 us
    unnamed x1, local copies, waits for them, and re-layouts  1.67 us

profile of v2, /device:TPU:24, one launch (start us, length us, event | category | flops | bytes accessed | tf_op | source)
XLA Modules:
  0.0 41.5 jit_solution(11302516790704975169)
XLA Ops:
  0.7 39.1 %shard_map.82 = bf16[128,1024]{1,0:T(8,128)(2,1)} custom-call(bf16[128,1024]{1,0:T(8,128)(2,1)} %bitcast.9, bf16[128,128]{1,0:T(8,128)(2,1)} %bitcast.12, bf16[128,128]{1,0:T(8,128)(2,1)} %bitcast.13, bf16[512,128]{1,0:T(8,128)(2,1)} %bitcast.10, bf16[512,128]{1,0:T(8,128)(2,1)} %bitcast.11, s32[1,32]{1,0:T(1,128)} %bitcast.14, s32[1,1]{1,0:T(1,128)S(6)} %copy.10.count_ref, ...), custom_call_target="tpu_custom_call" | custom-call | flops 2684354560 | bytes 1048576 | tf_op jit(solution)/shard_map/pallas_call | solution.py:408
  39.8 1.7 %copy.11 = bf16[1,128,1024]{2,1,0:T(8,128)(2,1)} copy(bf16[1,128,1024]{2,1,0:T(8,128)(2,1)} %bitcast.8) | data formatting | bytes 524288

commit v3 on v2

--- a/solution.py
+++ b/solution.py
@@ -57,7 +57,7 @@
     ncb = GROUP * part // BLK
     nqb = n * per
     rows_of_group = GROUP * tok
-    tile = min(2 * tok, rows_of_group)
+    tile = min(4 * tok, rows_of_group)
     outer = n // 2
     sec = lax.axis_index("section")
     me = lax.axis_index("seq")
@@ -270,6 +270,21 @@
                 relay(which, high, ACROSS).wait_recv()
             attend_cache(high)
 
+    partner = me + 1 - 2 * i
+    odd = o % 2
+
+    def crosses(which, k, parity):
+        return (k > 1) | (odd != parity) | (which != CV)
+
+    def lend(action):
+        @pl.when(odd == 0)
+        def _():
+            action(relay(CV, partner, UP))
+
+        @pl.when(odd == 1)
+        def _():
+            action(relay(CV, partner, DOWN))
+
     def step(k, carry):
         low, high = me - 2 * k, me + 2 * k
 
@@ -283,7 +298,9 @@
                     def _():
                         relay(which, low, UP).start()
 
-                    relay(which, low, ACROSS).start()
+                    @pl.when(crosses(which, k, 1))
+                    def _():
+                        relay(which, low, ACROSS).start()
 
         def pass_down(*arrays):
             @pl.when(o + k < outer)
@@ -295,12 +312,19 @@
                     def _():
                         relay(which, high, DOWN).start()
 
-                    relay(which, high, ACROSS).start()
+                    @pl.when(crosses(which, k, 0))
+                    def _():
+                        relay(which, high, ACROSS).start()
 
         pass_up(CK)
         pass_down(CK)
         pass_up(CV)
         pass_down(CV)
+        @pl.when(k == 1)
+        def _():
+            relay(CV, partner, ACROSS).wait_recv()
+            lend(lambda copy: copy.start())
+
         pass_up(SK, SV)
 
         @pl.when(k > 1)
@@ -309,9 +333,7 @@
 
         @pl.when(k == 1)
         def _():
-            partner = me + 1 - 2 * i
-            for which in (CK, CV):
-                relay(which, partner, ACROSS).wait_recv()
+            relay(CK, partner, ACROSS).wait_recv()
             attend_cache(partner)
 
             @pl.when(i == 1)
@@ -375,7 +397,9 @@
                 def _():
                     relay(which, low, UP).wait_send()
 
-                relay(which, low, ACROSS).wait_send()
+                @pl.when(crosses(which, k, 1))
+                def _():
+                    relay(which, low, ACROSS).wait_send()
 
         @pl.when(o + k < outer)
         def _():
@@ -385,10 +409,13 @@
                 def _():
                     relay(which, high, DOWN).wait_send()
 
-                relay(which, high, ACROSS).wait_send()
+                @pl.when(crosses(which, k, 0))
+                def _():
+                    relay(which, high, ACROSS).wait_send()
 
         return carry
 
+    lend(lambda copy: copy.wait_send())
     lax.fori_loop(1, outer, drain, 0)
 
 

time: 41.6 us -> 42.1 us (1.012)
  the two profiles are of different devices: /device:TPU:24 before, /device:TPU:0 now
where the time goes in v3:
time: 42.1 us; the launch traced here: 41.9 us
  Pallas kernels  39.6 us (94%)
  local copies, waits for them, and re-layouts  1.67 us (4%)
  between operations  0.66 us (2%)
    pallas_call x1, Pallas kernels, per_device(): pl.pallas_call(functools.partial(kernel, layers, n), out_shape=jax.ShapeD...  39.6 us
    unnamed x1, local copies, waits for them, and re-layouts  1.67 us

profile of v3, /device:TPU:0, one launch (start us, length us, event | category | flops | bytes accessed | tf_op | source)
XLA Modules:
  0.0 41.9 jit_solution(3175587401688270455)
XLA Ops:
  0.7 39.6 %shard_map.82 = bf16[128,1024]{1,0:T(8,128)(2,1)} custom-call(bf16[128,1024]{1,0:T(8,128)(2,1)} %bitcast.9, bf16[128,128]{1,0:T(8,128)(2,1)} %bitcast.12, bf16[128,128]{1,0:T(8,128)(2,1)} %bitcast.13, bf16[512,128]{1,0:T(8,128)(2,1)} %bitcast.10, bf16[512,128]{1,0:T(8,128)(2,1)} %bitcast.11, s32[1,32]{1,0:T(1,128)} %bitcast.14, s32[1,1]{1,0:T(1,128)S(6)} %copy.10.count_ref, ...), custom_call_target="tpu_custom_call" | custom-call | flops 2684354560 | bytes 1048576 | tf_op jit(solution)/shard_map/pallas_call | solution.py:435
  40.3 1.7 %copy.11 = bf16[1,128,1024]{2,1,0:T(8,128)(2,1)} copy(bf16[1,128,1024]{2,1,0:T(8,128)(2,1)} %bitcast.8) | data formatting | bytes 524288

commit v4 on v3

--- a/solution.py
+++ b/solution.py
@@ -167,6 +167,144 @@
         def _():
             relay(which, me, ACROSS).start()
 
+    def attend(keys, values, first_block, base, diagonal=False):
+        width = keys.shape[0]
+        block = lax.broadcasted_iota(jnp.int32, (width, LANES), 0) // BLK + first_block
+        mark = lax.broadcasted_iota(jnp.int32, (width, LANES), 1) == block
+        keys = jnp.concatenate([keys, jnp.where(mark, 1.0, 0.0).astype(jnp.bfloat16)], axis=1)
+        values = jnp.concatenate([values, jnp.ones((width, LANES), jnp.bfloat16)], axis=1)
+        span = width // LANES
+
+        def scores_of(rows):
+            scores = lax.dot_general(
+                qaug[rows, :], keys, (((1,), (1,)), ((), ())), preferred_element_type=jnp.float32
+            )
+            if diagonal:
+                token = lax.rem(lax.broadcasted_iota(jnp.int32, (tile, width), 0), tok)
+                key = lax.broadcasted_iota(jnp.int32, (tile, width), 1)
+                scores = jnp.where(key <= token, scores, MASKED)
+            return scores
+
+        def update(rows, scores):
+            high = jnp.broadcast_to(jnp.max(scores, axis=1, keepdims=True), (tile, LANES))
+            if not diagonal:
+                old = top[rows, :]
+                high = jnp.maximum(old, high)
+            top[rows, :] = high
+            wide = jnp.concatenate([high] * span, axis=1)
+            weights = jnp.exp2((scores - wide) * scale).astype(jnp.bfloat16)
+            fresh = jnp.dot(weights, values, preferred_element_type=jnp.float32)
+            if diagonal:
+                acc[rows, :] = fresh
+            else:
+                factor = jnp.exp2((old - high) * scale)
+                acc[rows, :] = acc[rows, :] * jnp.concatenate([factor] * 2, axis=1) + fresh
+
+        spans = [
+            pl.ds(base + t * tile if kvh == 1 else pl.multiple_of(base + t * tile, tile), tile)
+            for t in range(rows_of_group // tile)
+        ]
+        ahead = scores_of(spans[0])
+        for t, rows in enumerate(spans):
+            scores = ahead
+            if t + 1 < len(spans):
+                ahead = scores_of(spans[t + 1])
+            update(rows, scores)
+
+    def attend_cache(slot):
+        attend(
+            ckbuf[slot],
+            cvbuf[slot],
+            lax.rem(slot, GROUP) * (part // BLK),
+            0 if kvh == 1 else slot // GROUP * rows_of_group,
+        )
+
+    def attend_stretch(slot, slots, diagonal=False):
+        for g in range(kvh):
+            keys = skbuf[pl.ds(slot, slots), :, g * HEAD : (g + 1) * HEAD]
+            values = svbuf[pl.ds(slot, slots), :, g * HEAD : (g + 1) * HEAD]
+            attend(
+                keys.reshape(slots * tok, HEAD),
+                values.reshape(slots * tok, HEAD),
+                ncb + slot * per,
+                g * rows_of_group,
+                diagonal,
+            )
+
+    def across(k):
+        low, high = me - 2 * k + 1 - 2 * i, me + 2 * k + 1 - 2 * i
+
+        @pl.when(o - k >= 0)
+        def _():
+            for which in (CK, CV, SK, SV):
+                relay(which, low, ACROSS).wait_recv()
+            attend_cache(low)
+            attend_stretch((o - k) * 2, 2)
+
+        @pl.when(o + k < outer)
+        def _():
+            for which in (CK, CV):
+                relay(which, high, ACROSS).wait_recv()
+            attend_cache(high)
+
+    partner = me + 1 - 2 * i
+    odd = o % 2
+
+    def crosses(which, k, parity):
+        return (k > 1) | (odd != parity) | (which != CV)
+
+    def lend(action):
+        @pl.when(odd == 0)
+        def _():
+            action(relay(CV, partner, UP))
+
+        @pl.when(odd == 1)
+        def _():
+            action(relay(CV, partner, DOWN))
+
+    def pass_up(k, *arrays):
+        low = me - 2 * k
+
+        @pl.when(o - k >= 0)
+        def _():
+            for which in arrays:
+                relay(which, low, UP).wait_recv()
+
+                @pl.when(o < outer - 1)
+                def _():
+                    relay(which, low, UP).start()
+
+                @pl.when(crosses(which, k, 1))
+                def _():
+                    relay(which, low, ACROSS).start()
+
+    def pass_down(k, *arrays):
+        high = me + 2 * k
+
+        @pl.when(o + k < outer)
+        def _():
+            for which in arrays:
+                relay(which, high, DOWN).wait_recv()
+
+                @pl.when(o > 0)
+                def _():
+                    relay(which, high, DOWN).start()
+
+                @pl.when(crosses(which, k, 0))
+                def _():
+                    relay(which, high, ACROSS).start()
+
+    def along(k):
+        @pl.when(o - k >= 0)
+        def _():
+            attend_cache(me - 2 * k)
+
+        @pl.when(o + k < outer)
+        def _():
+            attend_cache(me + 2 * k)
+
+    pass_up(1, CK)
+    pass_down(1, CK)
     shifts[2].wait_recv()
     for d in range(1, n):
         src = lax.rem(me + d, n)
@@ -185,174 +323,36 @@
                 tabr[h, j].astype(jnp.bfloat16), (BLK, LANES)
             )
 
-    def attend(keys, values, first_block, base, diagonal=False):
-        width = keys.shape[0]
-        block = lax.broadcasted_iota(jnp.int32, (width, LANES), 0) // BLK + first_block
-        mark = lax.broadcasted_iota(jnp.int32, (width, LANES), 1) == block
-        keys = jnp.concatenate([keys, jnp.where(mark, 1.0, 0.0).astype(jnp.bfloat16)], axis=1)
-        values = jnp.concatenate([values, jnp.ones((width, LANES), jnp.bfloat16)], axis=1)
-        span = width // LANES
-
-        def scores_of(rows):
-            scores = lax.dot_general(
-                qaug[rows, :], keys, (((1,), (1,)), ((), ())), preferred_element_type=jnp.float32
-            )
-            if diagonal:
-                token = lax.rem(lax.broadcasted_iota(jnp.int32, (tile, width), 0), tok)
-                key = lax.broadcasted_iota(jnp.int32, (tile, width), 1)
-                scores = jnp.where(key <= token, scores, MASKED)
-            return scores
-
-        def update(rows, scores):
-            high = jnp.broadcast_to(jnp.max(scores, axis=1, keepdims=True), (tile, LANES))
-            if not diagonal:
-                old = top[rows, :]
-                high = jnp.maximum(old, high)
-            top[rows, :] = high
-            wide = jnp.concatenate([high] * span, axis=1)
-            weights = jnp.exp2((scores - wide) * scale).astype(jnp.bfloat16)
-            fresh = jnp.dot(weights, values, preferred_element_type=jnp.float32)
-            if diagonal:
-                acc[rows, :] = fresh
-            else:
-                factor = jnp.exp2((old - high) * scale)
-                acc[rows, :] = acc[rows, :] * jnp.concatenate([factor] * 2, axis=1) + fresh
-
-        spans = [
-            pl.ds(base + t * tile if kvh == 1 else pl.multiple_of(base + t * tile, tile), tile)
-            for t in range(rows_of_group // tile)
-        ]
-        ahead = scores_of(spans[0])
-        for t, rows in enumerate(spans):
-            scores = ahead
-            if t + 1 < len(spans):
-                ahead = scores_of(spans[t + 1])
-            update(rows, scores)
-
-    def attend_cache(slot):
-        attend(
-            ckbuf[slot],
-            cvbuf[slot],
-            lax.rem(slot, GROUP) * (part // BLK),
-            0 if kvh == 1 else slot // GROUP * rows_of_group,
-        )
-
-    def attend_stretch(slot, slots, diagonal=False):
-        for g in range(kvh):
-            keys = skbuf[pl.ds(slot, slots), :, g * HEAD : (g + 1) * HEAD]
-            values = svbuf[pl.ds(slot, slots), :, g * HEAD : (g + 1) * HEAD]
-            attend(
-                keys.reshape(slots * tok, HEAD),
-                values.reshape(slots * tok, HEAD),
-                ncb + slot * per,
-                g * rows_of_group,
-                diagonal,
-            )
-
+    pass_up(1, CV)
+    pass_down(1, CV)
     attend_stretch(me, 1, diagonal=True)
+    relay(CV, partner, ACROSS).wait_recv()
+    lend(lambda copy: copy.start())
+    pass_up(1, SK, SV)
     for copy in locals_:
         copy.wait()
     attend_cache(me)
-
-    def across(k):
-        low, high = me - 2 * k + 1 - 2 * i, me + 2 * k + 1 - 2 * i
-
-        @pl.when(o - k >= 0)
-        def _():
-            for which in (CK, CV, SK, SV):
-                relay(which, low, ACROSS).wait_recv()
-            attend_cache(low)
-            attend_stretch((o - k) * 2, 2)
-
-        @pl.when(o + k < outer)
-        def _():
-            for which in (CK, CV):
-                relay(which, high, ACROSS).wait_recv()
-            attend_cache(high)
-
-    partner = me + 1 - 2 * i
-    odd = o % 2
-
-    def crosses(which, k, parity):
-        return (k > 1) | (odd != parity) | (which != CV)
-
-    def lend(action):
-        @pl.when(odd == 0)
-        def _():
-            action(relay(CV, partner, UP))
-
-        @pl.when(odd == 1)
-        def _():
-            action(relay(CV, partner, DOWN))
+    relay(CK, partner, ACROSS).wait_recv()
+    attend_cache(partner)
+
+    @pl.when(i == 1)
+    def _():
+        for which in (SK, SV):
+            relay(which, partner, ACROSS).wait_recv()
+        attend_stretch(partner, 1)
 
     def step(k, carry):
-        low, high = me - 2 * k, me + 2 * k
-
-        def pass_up(*arrays):
-            @pl.when(o - k >= 0)
-            def _():
-                for which in arrays:
-                    relay(which, low, UP).wait_recv()
-
-                    @pl.when(o < outer - 1)
-                    def _():
-                        relay(which, low, UP).start()
-
-                    @pl.when(crosses(which, k, 1))
-                    def _():
-                        relay(which, low, ACROSS).start()
-
-        def pass_down(*arrays):
-            @pl.when(o + k < outer)
-            def _():
-                for which in arrays:
-                    relay(which, high, DOWN).wait_recv()
-
-                    @pl.when(o > 0)
-                    def _():
-                        relay(which, high, DOWN).start()
-
-                    @pl.when(crosses(which, k, 0))
-                    def _():
-                        relay(which, high, ACROSS).start()
-
-        pass_up(CK)
-        pass_down(CK)
-        pass_up(CV)
-        pass_down(CV)
-        @pl.when(k == 1)
-        def _():
-            relay(CV, partner, ACROSS).wait_recv()
-            lend(lambda copy: copy.start())
-
-        pass_up(SK, SV)
-
-        @pl.when(k > 1)
-        def _():
-            across(k - 1)
-
-        @pl.when(k == 1)
-        def _():
-            relay(CK, partner, ACROSS).wait_recv()
-            attend_cache(partner)
-
-            @pl.when(i == 1)
-            def _():
-                for which in (SK, SV):
-                    relay(which, partner, ACROSS).wait_recv()
-                attend_stretch(partner, 1)
-
-        @pl.when(o - k >= 0)
-        def _():
-            attend_cache(low)
-
-        @pl.when(o + k < outer)
-        def _():
-            attend_cache(high)
-
+        along(k - 1)
+        pass_up(k, CK)
+        pass_down(k, CK)
+        pass_up(k, CV)
+        pass_down(k, CV)
+        pass_up(k, SK, SV)
+        across(k - 1)
         return carry
 
-    lax.fori_loop(1, outer, step, 0)
+    lax.fori_loop(2, outer, step, 0)
+    along(outer - 1)
     across(outer - 1)
 
     for h in range(n):
@@ -434,7 +434,7 @@
         keys_all = GROUP * part + n * tok
         result = pl.pallas_call(
             functools.partial(kernel, layers, n),
-            out_shape=jax.ShapeDtypeStruct((tok, wide), dtype),
+            out_shape=pltpu.VMEM((tok, wide), dtype),
             in_specs=[anywhere] * 5 + [scalars] * 3,
             out_specs=pl.BlockSpec(memory_space=pltpu.VMEM),
             scratch_shapes=[
@@ -457,7 +457,7 @@
                 pltpu.SemaphoreType.DMA((n,)),
             ],
             compiler_params=pltpu.CompilerParams(
-                collective_id=0, has_side_effects=True, vmem_limit_bytes=63 * 2**20
+                collective_id=0, has_side_effects=True, vmem_limit_bytes=60 * 2**20
             ),
             cost_estimate=pl.CostEstimate(
                 flops=4 * rows * keys_all * HEAD,

time: 42.1 us -> 37.8 us (0.90)
  the two profiles are of different devices: /device:TPU:0 before, /device:TPU:24 now
where the time goes in v4:
time: 37.8 us; the launch traced here: 37.6 us
  Pallas kernels  36.2 us (96%)
  local copies, waits for them, and re-layouts  0.71 us (2%)
  between operations  0.66 us (2%)
    pallas_call x1, Pallas kernels, per_device(): pl.pallas_call(functools.partial(kernel, layers, n), out_shape=pltpu.VMEM...  36.2 us

profile of v4, /device:TPU:24, one launch (start us, length us, event | category | flops | bytes accessed | tf_op | source)
XLA Modules:
  0.0 37.6 jit_solution(9704320971542846756)
XLA Ops:
  0.7 36.2 %shard_map.82 = bf16[128,1024]{1,0:T(8,128)(2,1)S(1)} custom-call(bf16[128,1024]{1,0:T(8,128)(2,1)} %bitcast.9, bf16[128,128]{1,0:T(8,128)(2,1)} %bitcast.12, bf16[128,128]{1,0:T(8,128)(2,1)} %bitcast.13, bf16[512,128]{1,0:T(8,128)(2,1)} %bitcast.10, bf16[512,128]{1,0:T(8,128)(2,1)} %bitcast.11, s32[1,32]{1,0:T(1,128)} %bitcast.14, ...), custom_call_target="tpu_custom_call" | custom-call | flops 2684354560 | bytes 1048576 | tf_op jit(solution)/shard_map/pallas_call | solution.py:435
  36.9 0.7 %copy.10 = bf16[1,128,1024]{2,1,0:T(8,128)(2,1)} copy(bf16[1,128,1024]{2,1,0:T(8,128)(2,1)S(1)} %bitcast.8) | data formatting | bytes 524288

commit v5 on v4

--- a/solution.py
+++ b/solution.py
@@ -236,31 +236,55 @@
 
         @pl.when(o - k >= 0)
         def _():
-            for which in (CK, CV, SK, SV):
+            for which in (SK, SV):
                 relay(which, low, ACROSS).wait_recv()
+            attend_stretch((o - k) * 2, 2)
+            relay(CK, low, ACROSS).wait_recv()
+
+            @pl.when(o != k)
+            def _():
+                relay(CV, low, ACROSS).wait_recv()
+
             attend_cache(low)
-            attend_stretch((o - k) * 2, 2)
 
         @pl.when(o + k < outer)
         def _():
-            for which in (CK, CV):
-                relay(which, high, ACROSS).wait_recv()
+            relay(CK, high, ACROSS).wait_recv()
+
+            @pl.when(o + k != outer - 1)
+            def _():
+                relay(CV, high, ACROSS).wait_recv()
+
             attend_cache(high)
 
     partner = me + 1 - 2 * i
-    odd = o % 2
-
-    def crosses(which, k, parity):
-        return (k > 1) | (odd != parity) | (which != CV)
+    lent_low, lent_high = 1 - i, 2 * (outer - 1) + 1 - i
 
     def lend(action):
-        @pl.when(odd == 0)
+        @pl.when(o == 0)
         def _():
             action(relay(CV, partner, UP))
 
-        @pl.when(odd == 1)
+        @pl.when(o == outer - 1)
         def _():
             action(relay(CV, partner, DOWN))
+
+    def pass_lent(k):
+        @pl.when(o == k)
+        def _():
+            relay(CV, lent_low, UP).wait_recv()
+
+            @pl.when(o < outer - 1)
+            def _():
+                relay(CV, lent_low, UP).start()
+
+        @pl.when(o + k == outer - 1)
+        def _():
+            relay(CV, lent_high, DOWN).wait_recv()
+
+            @pl.when(o > 0)
+            def _():
+                relay(CV, lent_high, DOWN).start()
 
     def pass_up(k, *arrays):
         low = me - 2 * k
@@ -274,7 +298,7 @@
                 def _():
                     relay(which, low, UP).start()
 
-                @pl.when(crosses(which, k, 1))
+                @pl.when((which != CV) | (o != k))
                 def _():
                     relay(which, low, ACROSS).start()
 
@@ -290,7 +314,7 @@
                 def _():
                     relay(which, high, DOWN).start()
 
-                @pl.when(crosses(which, k, 0))
+                @pl.when((which != CV) | (o + k != outer - 1))
                 def _():
                     relay(which, high, ACROSS).start()
 
@@ -343,16 +367,18 @@
 
     def step(k, carry):
         along(k - 1)
+        pass_lent(k - 1)
         pass_up(k, CK)
         pass_down(k, CK)
+        pass_up(k, SK, SV)
         pass_up(k, CV)
         pass_down(k, CV)
-        pass_up(k, SK, SV)
         across(k - 1)
         return carry
 
     lax.fori_loop(2, outer, step, 0)
     along(outer - 1)
+    pass_lent(outer - 1)
     across(outer - 1)
 
     for h in range(n):
@@ -397,7 +423,7 @@
                 def _():
                     relay(which, low, UP).wait_send()
 
-                @pl.when(crosses(which, k, 1))
+                @pl.when((which != CV) | (o != k))
                 def _():
                     relay(which, low, ACROSS).wait_send()
 
@@ -409,13 +435,19 @@
                 def _():
                     relay(which, high, DOWN).wait_send()
 
-                @pl.when(crosses(which, k, 0))
+                @pl.when((which != CV) | (o + k != outer - 1))
                 def _():
                     relay(which, high, ACROSS).wait_send()
 
         return carry
 
     lend(lambda copy: copy.wait_send())
+
+    @pl.when((o > 0) & (o < outer - 1))
+    def _():
+        relay(CV, lent_low, UP).wait_send()
+        relay(CV, lent_high, DOWN).wait_send()
+
     lax.fori_loop(1, outer, drain, 0)
 
 

time: 37.8 us -> 35.7 us (0.944)
  the two profiles are of different devices: /device:TPU:24 before, /device:TPU:0 now
where the time goes in v5:
time: 35.7 us; the launch traced here: 35.6 us
  Pallas kernels  34.2 us (96%)
  local copies, waits for them, and re-layouts  0.71 us (2%)
  between operations  0.66 us (2%)
    pallas_call x1, Pallas kernels, per_device(): pl.pallas_call(functools.partial(kernel, layers, n), out_shape=pltpu.VMEM...  34.2 us

profile of v5, /device:TPU:0, one launch (start us, length us, event | category | flops | bytes accessed | tf_op | source)
XLA Modules:
  0.0 35.6 jit_solution(14202047620878465901)
XLA Ops:
  0.7 34.2 %shard_map.82 = bf16[128,1024]{1,0:T(8,128)(2,1)S(1)} custom-call(bf16[128,1024]{1,0:T(8,128)(2,1)} %bitcast.9, bf16[128,128]{1,0:T(8,128)(2,1)} %bitcast.12, bf16[128,128]{1,0:T(8,128)(2,1)} %bitcast.13, bf16[512,128]{1,0:T(8,128)(2,1)} %bitcast.10, bf16[512,128]{1,0:T(8,128)(2,1)} %bitcast.11, s32[1,32]{1,0:T(1,128)} %bitcast.14, ...), custom_call_target="tpu_custom_call" | custom-call | flops 2684354560 | bytes 1048576 | tf_op jit(solution)/shard_map/pallas_call | solution.py:467
  34.9 0.7 %copy.10 = bf16[1,128,1024]{2,1,0:T(8,128)(2,1)} copy(bf16[1,128,1024]{2,1,0:T(8,128)(2,1)S(1)} %bitcast.8) | data formatting | bytes 524288

commit v6 on v5

--- a/solution.py
+++ b/solution.py
@@ -156,17 +156,6 @@
         table(d).start()
     tabr[me] = tabs[pl.ds(me * per, per)]
 
-    for which in (SK, SV):
-        relay(which, me, UP).wait_recv()
-
-        @pl.when(o < outer - 1)
-        def _():
-            relay(which, me, UP).start()
-
-        @pl.when(i == 0)
-        def _():
-            relay(which, me, ACROSS).start()
-
     def attend(keys, values, first_block, base, diagonal=False):
         width = keys.shape[0]
         block = lax.broadcasted_iota(jnp.int32, (width, LANES), 0) // BLK + first_block
@@ -329,6 +318,19 @@
 
     pass_up(1, CK)
     pass_down(1, CK)
+    for which in (SK, SV):
+        relay(which, me, UP).wait_recv()
+
+        @pl.when(o < outer - 1)
+        def _():
+            relay(which, me, UP).start()
+
+        @pl.when(i == 0)
+        def _():
+            relay(which, me, ACROSS).start()
+
+    pass_up(1, CV)
+    pass_down(1, CV)
     shifts[2].wait_recv()
     for d in range(1, n):
         src = lax.rem(me + d, n)
@@ -347,8 +349,6 @@
                 tabr[h, j].astype(jnp.bfloat16), (BLK, LANES)
             )
 
-    pass_up(1, CV)
-    pass_down(1, CV)
     attend_stretch(me, 1, diagonal=True)
     relay(CV, partner, ACROSS).wait_recv()
     lend(lambda copy: copy.start())

time: 35.7 us -> 36.3 us (1.017)
  Pallas kernels: 34.2 us -> 34.8 us
    pallas_call x1, Pallas kernels: 34.2 us -> 34.8 us  [per_device(): pl.pallas_call(functools.partial(kernel, layers, n), out_shape=pltpu.VMEM...]
where the time goes in v6:
time: 36.3 us; the launch traced here: 36.1 us
  Pallas kernels  34.8 us (96%)
  local copies, waits for them, and re-layouts  0.71 us (2%)
  between operations  0.66 us (2%)
    pallas_call x1, Pallas kernels, per_device(): pl.pallas_call(functools.partial(kernel, layers, n), out_shape=pltpu.VMEM...  34.8 us

profile of v6, /device:TPU:0, one launch (start us, length us, event | category | flops | bytes accessed | tf_op | source)
XLA Modules:
  0.0 36.1 jit_solution(9637954833608825138)
XLA Ops:
  0.7 34.8 %shard_map.82 = bf16[128,1024]{1,0:T(8,128)(2,1)S(1)} custom-call(bf16[128,1024]{1,0:T(8,128)(2,1)} %bitcast.9, bf16[128,128]{1,0:T(8,128)(2,1)} %bitcast.12, bf16[128,128]{1,0:T(8,128)(2,1)} %bitcast.13, bf16[512,128]{1,0:T(8,128)(2,1)} %bitcast.10, bf16[512,128]{1,0:T(8,128)(2,1)} %bitcast.11, s32[1,32]{1,0:T(1,128)} %bitcast.14, ...), custom_call_target="tpu_custom_call" | custom-call | flops 2684354560 | bytes 1048576 | tf_op jit(solution)/shard_map/pallas_call | solution.py:467
  35.4 0.7 %copy.10 = bf16[1,128,1024]{2,1,0:T(8,128)(2,1)} copy(bf16[1,128,1024]{2,1,0:T(8,128)(2,1)S(1)} %bitcast.8) | data formatting | bytes 524288

commit v7 on v5

--- a/solution.py
+++ b/solution.py
@@ -57,7 +57,7 @@
     ncb = GROUP * part // BLK
     nqb = n * per
     rows_of_group = GROUP * tok
-    tile = min(4 * tok, rows_of_group)
+    tile = min(2 * tok, rows_of_group)
     outer = n // 2
     sec = lax.axis_index("section")
     me = lax.axis_index("seq")

time: 35.7 us -> 36 us (level)
  no operation moved by 1% of the time
where the time goes in v7:
time: 36 us; the launch traced here: 35.8 us
  Pallas kernels  34.4 us (96%)
  local copies, waits for them, and re-layouts  0.71 us (2%)
  between operations  0.66 us (2%)
    pallas_call x1, Pallas kernels, per_device(): pl.pallas_call(functools.partial(kernel, layers, n), out_shape=pltpu.VMEM...  34.4 us

profile of v7, /device:TPU:0, one launch (start us, length us, event | category | flops | bytes accessed | tf_op | source)
XLA Modules:
  0.0 35.8 jit_solution(9083584083776027054)
XLA Ops:
  0.7 34.4 %shard_map.82 = bf16[128,1024]{1,0:T(8,128)(2,1)S(1)} custom-call(bf16[128,1024]{1,0:T(8,128)(2,1)} %bitcast.9, bf16[128,128]{1,0:T(8,128)(2,1)} %bitcast.12, bf16[128,128]{1,0:T(8,128)(2,1)} %bitcast.13, bf16[512,128]{1,0:T(8,128)(2,1)} %bitcast.10, bf16[512,128]{1,0:T(8,128)(2,1)} %bitcast.11, s32[1,32]{1,0:T(1,128)} %bitcast.14, ...), custom_call_target="tpu_custom_call" | custom-call | flops 2684354560 | bytes 1048576 | tf_op jit(solution)/shard_map/pallas_call | solution.py:467
  35.1 0.7 %copy.10 = bf16[1,128,1024]{2,1,0:T(8,128)(2,1)} copy(bf16[1,128,1024]{2,1,0:T(8,128)(2,1)S(1)} %bitcast.8) | data formatting | bytes 524288
